TPU v7x, 128 devices: a whole 4x4x4 slice. The times are simulated.
128 devices in a mesh: row: 8 (over z, core), col: 16 (over y, x).
Axes of the slice: x: 4, y: 4, z: 4, core: 2. Of those that a mesh axis runs over, the one named last changes fastest.
Arguments:
- working: float32 [8, 8, 256, 4, 16, 256], P(None, 'row', None, None, 'col'), may hold values from -6 to 6
- factor_panel: float32 [2, 8, 8, 256, 256], P(None, None, 'row'), may hold values from -0.12 to 2, as said below
Outputs:
- gram_part: float32 [8, 8, 256, 4, 16, 256], P(None, 'row', None, None, 'col')
- finished_columns: float32 [4, 8, 256, 16, 8, 128], P(None, None, None, 'col', 'row')
Inputs may be any that keep to these rules, and one draw needn't show every extreme that they name: factor_panel holds a lower-triangular factor: entries above the factor's diagonal are zero and its diagonal entries lie between 1 and 2.
All inputs are finite; a program needn't handle non-finite values.
Results may differ from a plain program's by a relative error of at most 0.0001.
Values sent between devices are 32-bit elements; how exact they have to be, the bound alone decides.
A program may use at most 192 MiB of HBM per device.

v0:
```python
import jax
import jax.numpy as jnp
from jax import lax
from jax.sharding import PartitionSpec as P

BLK = 256
K = 30
STEPS = 2


def picked(value, axis, root):
    return lax.dynamic_index_in_dim(lax.all_gather(value, axis), root, 0, keepdims=False)


def per_device(working, factor_panel):
    row_count = lax.axis_size("row")
    col_count = lax.axis_size("col")
    row_index = lax.axis_index("row")
    blocks_rows = working.shape[0]
    width = working.shape[2]
    blocks_cols = working.shape[3]
    matrix_rows = working.reshape(blocks_rows, width, blocks_cols * width)
    global_block = jnp.arange(blocks_rows) * row_count + row_index

    def solve_row(slab, step_index):
        target = K + step_index
        owner = target % row_count
        diagonal = jnp.tril(factor_panel[step_index, target // row_count, 0])
        diagonal = jnp.where(row_index == owner, diagonal, jnp.eye(width, dtype=jnp.float32))
        solved = lax.linalg.triangular_solve(diagonal, slab, left_side=True, lower=True)
        return picked(solved, "row", owner)

    def eliminate(rows_part, blocks_part, column_part, solved, step_index):
        target = K + step_index
        updated = rows_part - jnp.einsum(
            "rab,bc->rac", column_part, solved, precision=lax.Precision.HIGHEST
        )
        below = (blocks_part > target)[:, None, None]
        here = (blocks_part == target)[:, None, None]
        return jnp.where(below, updated, jnp.where(here, solved[None], rows_part))

    solved_list = []
    solved = solve_row(matrix_rows[K // row_count], 0)
    for step_index in range(STEPS):
        solved_list.append(solved)
        if step_index + 1 < STEPS:
            slot = (K + step_index + 1) // row_count
            next_slab = eliminate(
                matrix_rows[slot : slot + 1],
                global_block[slot : slot + 1],
                factor_panel[step_index, slot : slot + 1, 0],
                solved,
                step_index,
            )
            following = solve_row(next_slab[0], step_index + 1)
        matrix_rows = eliminate(
            matrix_rows, global_block, factor_panel[step_index, :, 0], solved, step_index
        )
        if step_index + 1 < STEPS:
            solved = following
    stacked = jnp.concatenate(solved_list, 0)
    depth = stacked.shape[0]
    owners_count = col_count // row_count
    gathered = lax.all_gather(
        stacked.reshape(depth, blocks_cols, 1, width), "col", axis=2, tiled=True
    )
    gathered = gathered.reshape(depth, blocks_cols, owners_count, row_count, width)
    chosen = lax.dynamic_index_in_dim(gathered, row_index, 3, keepdims=False)
    row_panels = chosen.reshape(depth, blocks_rows * width)
    gram = lax.dot_general(
        row_panels, stacked, (((0,), (0,)), ((), ())), precision=lax.Precision.HIGHEST
    )
    gram = (gram * (1.0 / (STEPS * BLK))).reshape(blocks_rows, 1, width, blocks_cols, 1, width)
    finished_count = (K + STEPS) // row_count
    finished = matrix_rows[:finished_count].reshape(finished_count, 1, width, 1, row_count, -1)
    moved = lax.all_to_all(finished, "row", split_axis=4, concat_axis=1, tiled=True)
    return (gram, moved)


def solution(mesh):
    placed = (P(None, "row", None, None, "col", None), P(None, None, "row", None, None))
    return jax.shard_map(
        per_device,
        mesh=mesh,
        in_specs=placed,
        out_specs=(
            P(None, "row", None, None, "col", None),
            P(None, None, None, "col", "row", None),
        ),
        check_vma=False,
    )
```

profile of v0, /device:TPU:32, one launch (start us, length us, event | category | flops | bytes accessed | tf_op | source)
XLA Modules:
  0.0 432.9 jit_solution(2634957382837194387)
XLA Ops:
  7.2 1.1 fusion.16
  8.4 3.8 while.4
  8.4 0.6 fusion.36
  9.0 1.3 bitcast_dynamic-update-slice_fusion.4
  10.3 0.6 fusion.36
  10.9 1.3 bitcast_dynamic-update-slice_fusion.4
  12.2 19.7 %custom-call.4 = f32[2,128,128]{1,2,0:T(8,128)S(1)} custom-call(f32[2,128,128]{2,1,0:T(8,128)S(1)} %get-tuple-element.17), custom_call_target="InvertDiagBlocksLowerTriangular" | custom-call | tf_op jit(solution)/shard_map/triangular_solve/custom-call.1 | solution.py:30
  31.9 4.2 slice_reduce_fusion
  36.3 0.6 fusion.13
  36.9 0.6 convolution_subtract_fusion.1
  37.5 0.6 fusion.22
  38.1 1.0 pad_maximum_fusion.1
  39.2 0.6 all-gather.10.cloned.1.call-start
  39.8 0.6 slice.46
  41.7 0.5 slice.47
  42.2 4.1 while.5
  42.2 0.7 fusion.37
  42.9 1.3 bitcast_dynamic-update-slice_fusion.5
  44.3 0.7 fusion.37
  44.9 1.3 bitcast_dynamic-update-slice_fusion.5
  46.3 19.7 %custom-call.5 = f32[2,128,128]{1,2,0:T(8,128)S(1)} custom-call(f32[2,128,128]{2,1,0:T(8,128)S(1)} %get-tuple-element.18), custom_call_target="InvertDiagBlocksLowerTriangular" | custom-call | tf_op jit(solution)/shard_map/triangular_solve/custom-call.1 | solution.py:30
  66.0 24.4 %all-gather.8.cloned.1.call-done = f32[2048,1024]{1,0:T(8,128)} async-done(((f32[256,1024]{1,0:T(8,128)}), f32[2048,1024]{1,0:T(8,128)}) %all-gather.8.cloned.1.call-update) | async-done | bytes 8388624 | tf_op jit(solution)/shard_map/all_gather | solution.py:12
  90.4 2.8 fusion.8
  93.3 0.6 fusion.11
  93.9 0.6 convolution_subtract_fusion
  94.5 0.6 fusion.20
  95.1 1.0 pad_maximum_fusion.2
  96.4 1.3 slice.86
  97.7 0.5 concatenate.13
  98.2 1.2 copy.38
  99.4 47.1 %all-gather.10.cloned.1.call-done = f32[2048,1024]{1,0:T(8,128)} async-done(((f32[256,1024]{1,0:T(8,128)}), f32[2048,1024]{1,0:T(8,128)}) %all-gather.10.cloned.1.call-update) | async-done | bytes 8388624 | tf_op jit(solution)/shard_map/all_gather | solution.py:12
  146.5 1.3 slice.92
  148.5 2.8 pad_maximum_fusion
  151.3 20.9 %copy.42 = f32[8,1,256,4,1,256]{2,5,3,0,4,1:T(8,128)} copy(f32[8,1,256,4,1,256]{5,4,3,2,1,0:T(1,128)} %param.4) | data formatting | bytes 16777216 | tf_op args[0]
  172.5 17.2 %convolution_bitcast_fusion.1 = f32[8,256,1024]{1,2,0:T(8,128)} fusion(f32[2,8,1,256,256]{4,3,1,2,0:T(8,128)} %bitcast.110, f32[2048,1024]{1,0:T(8,128)} %all-gather.8.cloned.1.call-done), kind=kOutput, calls=%fused_computation.11 | convolution fusion | flops 6442450944 | bytes 11534336 | tf_op jit(solution)/shard_map/rab,bc->rac/dot_general | solution.py:35
  189.8 1.3 copy.48
  191.1 16.6 %convolution_bitcast_fusion = f32[8,256,1024]{1,2,0:T(8,128)S(1)} fusion(f32[2,8,1,256,256]{4,3,1,2,0:T(8,128)} %bitcast.111, f32[2048,1024]{1,0:T(8,128)} %all-gather.10.cloned.1.call-done), kind=kOutput, calls=%fused_computation.10 | convolution fusion | flops 6442450944 | bytes 11534336 | tf_op jit(solution)/shard_map/rab,bc->rac/dot_general | solution.py:35
  207.7 4.5 %fusion = f32[4,256,1024]{1,2,0:T(8,128)} fusion(f32[8,256,1024]{1,2,0:T(8,128)S(1)} %convolution_bitcast_fusion, f32[8,256,1024]{1,2,0:T(8,128)S(1)} %copy-done, f32[8,256,1024]{1,2,0:T(8,128)} %bitcast.108, f32[256,1024]{0,1:T(8,128)S(1)} %copy-done.1, f32[256,1024]{0,1:T(8,128)S(1)} %copy.45, pred[4]{0:T(512)(128)(4,1)S(1)} %bitcast.117, ...), kind=kLoop, calls=%fused_computation.7 | loop fusion | flops 6291456 | bytes 18874384 | tf_op jit(solution)/shard_map/jit(_where)/select_n | solution.py:40
  212.2 5.9 %copy.49 = f32[4,1,256,1,8,128]{5,2,0,3,1,4:T(8,128)} copy(f32[4,1,256,1,8,128]{2,5,4,0,3,1:T(8,128)} %bitcast.109) | data formatting | bytes 8388608 | tf_op jit(solution)/shard_map/reshape | solution.py:75
  218.2 6.0 %all-to-all-start = ((f32[4,1,256,1,8,128]{5,2,0,3,1,4:T(8,128)}), f32[4,1,256,1,8,128]{5,2,0,3,1,4:T(8,128)}, u32[]{:S(2)}, u32[]{:S(2)}) async-start(f32[4,1,256,1,8,128]{5,2,0,3,1,4:T(8,128)} %copy.49), calls=%async_computation | async-start | bytes 8388608 | tf_op jit(solution)/shard_map/all_to_all | solution.py:76
  224.1 48.3 %all-to-all-done = f32[4,1,256,1,8,128]{5,2,0,3,1,4:T(8,128)} async-done(((f32[4,1,256,1,8,128]{5,2,0,3,1,4:T(8,128)}), f32[4,1,256,1,8,128]{5,2,0,3,1,4:T(8,128)}, u32[]{:S(2)}, u32[]{:S(2)}) %all-to-all-start) | async-done | bytes 4194336 | tf_op jit(solution)/shard_map/all_to_all | solution.py:76
  272.5 11.4 %copy.51 = f32[4,8,256,1,1,128]{5,4,3,2,1,0:T(1,128)} copy(f32[4,8,256,1,1,128]{5,2,0,1,4,3:T(8,128)} %bitcast.26) | data formatting | bytes 8388608
  283.9 65.5 %all-gather.6.cloned.1.call-done = f32[512,4,16,256]{3,0,1,2:T(8,128)} async-done(((f32[512,4,1,256]{3,0,1,2:T(8,128)}), f32[512,4,16,256]{3,0,1,2:T(8,128)}) %all-gather.6.cloned.1.call-update) | async-done | bytes 33554448 | tf_op jit(solution)/shard_map/all_gather | solution.py:64
  349.4 28.3 %copy.59 = f32[512,4,16,256]{3,2,1,0:T(8,128)S(1)} copy(f32[512,4,16,256]{3,0,1,2:T(8,128)} %all-gather.6.cloned.1.call-done) | data formatting | bytes 67108864 | tf_op jit(solution)/shard_map/all_gather | solution.py:64
  377.7 6.6 %constant_dynamic-slice_fusion.2 = f32[512,4,2,1,256]{4,3,2,1,0:T(1,128)} fusion(f32[512,4,2,8,256]{4,3,2,1,0:T(8,128)S(1)} %bitcast.106, s32[]{:T(128)S(6)} %select_n.57), kind=kLoop, calls=%fused_computation.59 | loop fusion | bytes 8388612 | tf_op jit(solution)/shard_map/jit(dynamic_index_in_dim)/dynamic_slice | solution.py:68
  384.3 10.9 %copy.41 = f32[512,4,2,1,256]{0,4,2,1,3:T(8,128)} copy(f32[512,4,2,1,256]{4,3,2,1,0:T(1,128)} %constant_dynamic-slice_fusion.2) | data formatting | bytes 8388608 | tf_op jit(solution)/shard_map/jit(dynamic_index_in_dim)/dynamic_slice | solution.py:68
  395.2 17.5 %convolution_multiply_fusion = f32[2048,1024]{1,0:T(8,128)} fusion(f32[512,2048]{0,1:T(8,128)} %bitcast.107, f32[256,1024]{1,0:T(8,128)S(1)} %slice.92, f32[256,1024]{1,0:T(8,128)S(1)} %slice.86), kind=kOutput, calls=%fused_computation.5 | convolution fusion | flops 12887523328 | bytes 14680064 | tf_op jit(solution)/shard_map/dot_general | solution.py:70
  412.7 13.5 %reshape.102 = f32[8,1,256,4,1,256]{5,4,3,2,1,0:T(1,128)} reshape(f32[2048,1024]{1,0:T(8,128)} %convolution_multiply_fusion) | data formatting | bytes 16777216 | tf_op jit(solution)/shard_map/reshape | solution.py:73
  (24 shorter events, 1.7 us)
Async XLA Ops:
  7.2 83.3 %all-gather.8.cloned.1.call-start = ((), (), s32[]{:S(2)}) async-start(), calls=%async_computation.2 | async-start | bytes 9437184 | tf_op jit(solution)/shard_map/all_gather | solution.py:12
  39.2 107.3 %all-gather.10.cloned.1.call-start = ((), (), s32[]{:S(2)}) async-start(), calls=%async_computation.3 | async-start | bytes 9437184 | tf_op jit(solution)/shard_map/all_gather | solution.py:12
  96.2 253.2 %all-gather.6.cloned.1.call-start = ((), (), s32[]{:S(2)}) async-start(), calls=%async_computation.1 | async-start | bytes 35651584 | tf_op jit(solution)/shard_map/all_gather | solution.py:64
  191.1 16.7 %copy-start = (f32[8,256,1024]{1,2,0:T(8,128)S(1)}, f32[8,256,1024]{1,2,0:T(8,128)}, u32[]{:S(2)}) copy-start(f32[8,256,1024]{1,2,0:T(8,128)} %convolution_bitcast_fusion.1) | copy-start | bytes 25165828
  191.1 16.7 %copy-start.1 = (f32[256,1024]{0,1:T(8,128)S(1)}, f32[256,1024]{0,1:T(8,128)}, u32[]{:S(2)}) copy-start(f32[256,1024]{0,1:T(8,128)} %copy.48) | copy-start | bytes 3145732
  218.2 54.3 %all-to-all-start = ((f32[4,1,256,1,8,128]{5,2,0,3,1,4:T(8,128)}), f32[4,1,256,1,8,128]{5,2,0,3,1,4:T(8,128)}, u32[]{:S(2)}, u32[]{:S(2)}) async-start(f32[4,1,256,1,8,128]{5,2,0,3,1,4:T(8,128)} %copy.49), calls=%async_computation | async-start | bytes 8388608 | tf_op jit(solution)/shard_map/all_to_all | solution.py:76
Sparse Core Ops, SparseCore 0:
  39.3 51.0 all-gather.7
  96.3 50.1 all-gather.9
  151.4 197.8 all-gather.5
where the time goes:
time: 441 us; the launch traced here: 433 us
  waiting for transfers between devices  185 us (42%)
  local copies, waits for them, and re-layouts  117 us (27%)
  matrix products  57.9 us (13%)
  other arithmetic  49.8 us (11%)
  between operations  15.5 us (4%)
  starting transfers between devices  6.78 us (2%)
    all_gather x2, waiting for transfers between devices, picked(): lax.all_gather(value, axis)  71.6 us
    all_gather x1, waiting for transfers between devices, per_device(): lax.all_gather(stacked.reshape(depth, blocks_cols, 1, width), 'col', axis...  65.5 us
    all_to_all x1, waiting for transfers between devices, per_device(): lax.all_to_all(finished, 'row', split_axis=4, concat_axis=1, tiled=True)  48.3 us
    another operation x6, other arithmetic, solve_row(): lax.linalg.triangular_solve(diagonal, slab, left_side=True, lower=True)  42.5 us
    dot_general x3, matrix products, eliminate(): jnp.einsum('rab,bc->rac', column_part, solved, precision=lax.Precision.HI...  36.7 us
    unnamed x7, local copies, waits for them, and re-layouts  32.5 us
    all_gather x1, local copies, waits for them, and re-layouts, per_device(): lax.all_gather(stacked.reshape(depth, blocks_cols, 1, width), 'col', axis...  28.3 us
    dynamic_slice x2, local copies, waits for them, and re-layouts, per_device(): chosen = lax.dynamic_index_in_dim(gathered, row_index, 3, keepdims=False)  17.6 us
  transfers between devices with their start and end apart: 4, of which 4 were waited for; matrix products, arithmetic and copies ran while one was open for 24% of the time, Pallas kernels for 0%

commit v1 on v0

v1 whole, which is shorter than its diff:
```python
import jax
import jax.numpy as jnp
from jax import lax
from jax.experimental import pallas as pl
from jax.experimental.pallas import tpu as pltpu
from jax.sharding import PartitionSpec as P

MESH = pl.DeviceIdType.MESH
F32 = jnp.float32
BF16 = jnp.bfloat16
BLK = 256
HALF = 128
NJ = 4
SLOT = 3
SCALE = 1.0 / 512


def full(a, b):
    return lax.dot_general(
        a, b, (((1,), (0,)), ((), ())), precision=lax.Precision.HIGHEST, preferred_element_type=F32
    )


def small_inverse(block):
    row = lax.broadcasted_iota(jnp.int32, (HALF, HALF), 0)
    col = lax.broadcasted_iota(jnp.int32, (HALF, HALF), 1)
    eye = row == col
    on_diagonal = jnp.where(eye, block, 0.0)
    inv_col = 1.0 / jnp.sum(on_diagonal, axis=1, keepdims=True)
    inv_row = 1.0 / jnp.sum(on_diagonal, axis=0, keepdims=True)
    first = (row == col + 1) & ((row & 1) == 1)
    inverse = jnp.where(eye, inv_col, jnp.where(first, -block * inv_col * inv_row, 0.0))
    shift = 1
    while (1 << shift) < HALF:
        below = ((row >> shift) & 1) == 1
        beside = (col >> shift) == (row >> shift) - 1
        lower = jnp.where(below & beside, block, 0.0)
        inverse = inverse - full(inverse, full(lower, inverse))
        shift += 1
    return inverse


def split(value):
    high = value.astype(BF16)
    low = (value - high.astype(F32)).astype(BF16)
    return high, low


def tdot(a, b):
    return lax.dot_general(a, b, (((0,), (0,)), ((), ())), preferred_element_type=F32)


def kernel(
    w_ref, f_ref, gram_ref, fin_ref,
    own, oth, panel, cross, high, low, stage, slab, diag, lower, inv,
    load_sem, a2a_send, a2a_recv, a2b_send, a2b_recv, local_sem,
    oth_send, oth_recv, own_send, own_recv, copy_sem,
    dir_send, panel_recv, cross_send, cross_recv, stage_sem,
):
    r = lax.axis_index("row")
    c = lax.axis_index("col")
    z, k = lax.div(r, 2), lax.rem(r, 2)
    y, x = lax.div(c, 4), lax.rem(c, 4)
    dx = lax.rem(x + 4 - 2 * lax.rem(z, 2), 4)
    dy = lax.rem(y + 4 - lax.div(z, 2), 4)
    other = (r + 1 - 2 * k, c)
    right = (r, 4 * y + lax.rem(x + 1, 4))
    left = (r, 4 * y + lax.rem(x + 3, 4))
    up = (r, 4 * lax.rem(y + 1, 4) + x)
    down = (r, 4 * lax.rem(y + 3, 4) + x)
    is_top = z == 3
    is_source = lax.div(lax.rem(c, 8), 2) == z
    source_panel = 2 * lax.rem(c, 2) + lax.div(c, 8)

    def remote(src, dst, send, recv, device):
        return pltpu.make_async_remote_copy(
            src, dst, send, recv, device_id=device, device_id_type=MESH
        )

    def loads():
        found = [pltpu.make_async_copy(f_ref.at[k, SLOT, 0], diag, load_sem.at[8])]
        found.append(pltpu.make_async_copy(f_ref.at[0, SLOT, 0], lower, load_sem.at[9]))
        for s in range(8):
            found.append(
                pltpu.make_async_copy(
                    w_ref.at[SLOT, :, s, 0, :], slab.at[s // 2, s % 2], load_sem.at[s]
                )
            )
        return found

    @pl.when(is_top)
    def _():
        for copy in loads():
            copy.start()

    barrier = pltpu.get_barrier_semaphore()
    for d in range(1, 8):
        pl.semaphore_signal(
            barrier, inc=1, device_id=(lax.rem(r + d, 8), c), device_id_type=MESH
        )
    for device in (right, left, up, down):
        pl.semaphore_signal(barrier, inc=1, device_id=device, device_id_type=MESH)
    pl.semaphore_wait(barrier, 11)

    def partner(d):
        return 2 * (z ^ (d >> 1)) + (k ^ (d & 1))

    def finished(d):
        t = partner(d)
        return remote(
            w_ref.at[pl.ds(0, 3), :, t],
            fin_ref.at[pl.ds(0, 3), r],
            a2a_send.at[d], a2a_recv.at[d], (t, c),
        )

    def finished_last(d):
        t = partner(d)
        return remote(
            w_ref.at[pl.ds(3, 1), :, t],
            fin_ref.at[pl.ds(3, 1), r],
            a2b_send.at[d], a2b_recv.at[d], (t, c),
        )

    for d in range(1, 8):
        finished(d).start()

        @pl.when(z < 3)
        def _():
            finished_last(d).start()

    own_rows = pltpu.make_async_copy(
        w_ref.at[pl.ds(0, 3), :, r], fin_ref.at[pl.ds(0, 3), r], local_sem.at[0]
    )
    own_last = pltpu.make_async_copy(
        w_ref.at[pl.ds(3, 1), :, r], fin_ref.at[pl.ds(3, 1), r], local_sem.at[1]
    )
    own_rows.start()

    @pl.when(z < 3)
    def _():
        own_last.start()

    @pl.when(is_top)
    def _():
        for copy in loads():
            copy.wait()
        top = small_inverse(diag[0:HALF, 0:HALF])
        bottom = small_inverse(diag[HALF:BLK, HALF:BLK])
        inv[0:HALF, 0:HALF] = top
        inv[0:HALF, HALF:BLK] = jnp.zeros((HALF, HALF), F32)
        inv[HALF:BLK, HALF:BLK] = bottom
        inv[HALF:BLK, 0:HALF] = -full(bottom, full(diag[HALF:BLK, 0:HALF], top))

    def to_other(j):
        return remote(own.at[j], oth.at[j], oth_send.at[j], oth_recv.at[j], other)

    def down_ring(j, target, sem):
        return remote(
            own.at[j], own.at[j], own_send.at[sem, j], own_recv.at[j], (2 * target + k, c)
        )

    def forwards_ring(j):
        return ((z == 0) & (j < 2)) | ((z == 2) & (j >= 2))

    def to_panel(j):
        return pltpu.make_async_copy(own.at[j], panel.at[source_panel, j], copy_sem.at[j])

    def solved_chunk(j):
        @pl.when(is_top)
        def _():
            @pl.when(k == 1)
            def _():
                to_other(j).wait_recv()
                for h in range(2):
                    slab[j, h] = slab[j, h] - full(lower[...], oth[j, h])

            for h in range(2):
                own[j, h] = full(inv[...], slab[j, h])

        @pl.when(z < 3)
        def _():
            down_ring(j, 1, 0).wait_recv()

        @pl.when(is_source)
        def _():
            to_panel(j).start()

        to_other(j).start()

        @pl.when(is_top)
        def _():
            down_ring(j, 0, 0).start()
            down_ring(j, 2, 1).start()

        @pl.when(forwards_ring(j))
        def _():
            down_ring(j, 1, 0).start()

        @pl.when(is_source)
        def _():
            to_panel(j).wait()

    near_x = ((dx == 1) | (dx == 2)).astype(jnp.int32)
    near_y = (dy == 2).astype(jnp.int32)

    def which(n):
        low_bit, high_bit = n & 1, n >> 1
        kp = jnp.where(k == 0, low_bit, high_bit) ^ near_x
        b = jnp.where(k == 0, high_bit, low_bit) ^ near_y
        return kp, b

    def hops(kp, b, j):
        p = 2 * kp + b
        odd = lax.rem(kp + j, 2)
        x_active = (k == 1) | (dy == 2 * b)
        y_active = (k == 0) | (dx == kp)
        goes = (
            x_active & ((dx == kp) | ((kp == 1) & (dx == 2))),
            x_active & ((dx == kp) | ((kp == 0) & (dx == 3))),
            y_active
            & (
                (dy == 2 * b)
                | ((odd == 0) & (dy == 1) & (b == 0))
                | ((odd == 1) & (dy == 3) & (b == 1))
            ),
            y_active
            & (
                (dy == 2 * b)
                | ((odd == 0) & (dy == 1) & (b == 1))
                | ((odd == 1) & (dy == 3) & (b == 0))
            ),
        )
        return [
            (
                go,
                remote(
                    panel.at[p, j], panel.at[p, j], dir_send.at[i, p, j], panel_recv.at[p, j], device
                ),
            )
            for i, (go, device) in enumerate(zip(goes, (right, left, up, down)))
        ]

    def to_cross(b, j):
        return remote(
            panel.at[2 * (1 - k) + b, j], cross.at[b, j], cross_send.at[b, j], cross_recv.at[b, j], other
        )

    def pass_on(n, j):
        kp, b = which(n)
        p = 2 * kp + b
        copies = hops(kp, b, j)

        @pl.when(jnp.logical_not(is_source & (source_panel == p)))
        def _():
            copies[0][1].wait_recv()

        for go, copy in copies:
            @pl.when(go)
            def _(copy=copy):
                copy.start()

        @pl.when(kp != k)
        def _():
            to_cross(b, j).start()

    def staged(i, s):
        slot = i & 1
        return pltpu.make_async_copy(
            stage.at[slot, s], gram_ref.at[i, :, s, 0, :], stage_sem.at[slot, s]
        )

    def split_columns():
        for j in range(NJ):
            @pl.when(jnp.logical_not(is_top & (k == 1)))
            def _(j=j):
                to_other(j).wait_recv()
            for h in range(2):
                s = 2 * j + h
                at = slice(HALF * s, HALF * (s + 1))
                high[0:BLK, at], low[0:BLK, at] = split(own[j, h])
                high[BLK:, at], low[BLK:, at] = split(oth[j, h])

    def gram_block(j, b):
        i = 2 * j + b
        to_cross(b, j).wait_recv()
        p = 2 * k + b
        mine = jnp.concatenate([panel[p, j, 0], panel[p, j, 1]], axis=1)
        theirs = jnp.concatenate([cross[b, j, 0], cross[b, j, 1]], axis=1)
        a_high, a_low = split(jnp.concatenate([mine, theirs], axis=0))

        @pl.when(i >= 2)
        def _():
            for s in range(8):
                staged(i, s).wait()

        for q in range(4):
            at = slice(BLK * q, BLK * (q + 1))
            b_high, b_low = high[:, at], low[:, at]
            value = (tdot(a_low, b_high) + tdot(a_high, b_low)) + tdot(a_high, b_high)
            value = value * SCALE
            stage[i & 1, 2 * q] = value[:, :HALF]
            stage[i & 1, 2 * q + 1] = value[:, HALF:]
            staged(i, 2 * q).start()
            staged(i, 2 * q + 1).start()

    def step(t, carry):
        @pl.when(t < 4)
        def _():
            solved_chunk(t)
            pass_on(0, t)
            pass_on(1, t)

        @pl.when((t >= 1) & (t < 5))
        def _():
            pass_on(2, t - 1)
            pass_on(3, t - 1)

        return carry

    lax.fori_loop(0, 5, step, 0)

    split_columns()
    last = [
        pltpu.make_async_copy(
            own.at[lax.div(r, 2), lax.rem(r, 2)], fin_ref.at[SLOT, 6 + k, :, 0, :], local_sem.at[2]
        ),
        pltpu.make_async_copy(
            oth.at[lax.div(r, 2), lax.rem(r, 2)], fin_ref.at[SLOT, 7 - k, :, 0, :], local_sem.at[3]
        ),
    ]
    for copy in last:
        copy.start()

    def product(j, carry):
        gram_block(j, 0)
        gram_block(j, 1)
        return carry

    lax.fori_loop(0, NJ, product, 0)

    for i in (6, 7):
        for s in range(8):
            staged(i, s).wait()
    for copy in last:
        copy.wait()
    own_rows.wait()

    @pl.when(z < 3)
    def _():
        own_last.wait()

    def close(j, carry):
        to_other(j).wait_send()

        @pl.when(is_top)
        def _():
            down_ring(j, 0, 0).wait_send()
            down_ring(j, 2, 1).wait_send()

        @pl.when(forwards_ring(j))
        def _():
            down_ring(j, 1, 0).wait_send()

        for kp in range(2):
            for b in range(2):
                for go, copy in hops(kp, b, j):
                    @pl.when(go)
                    def _(copy=copy):
                        copy.wait_send()
        for b in range(2):
            to_cross(b, j).wait_send()
        return carry

    lax.fori_loop(0, NJ, close, 0)
    for d in range(1, 8):
        finished(d).wait()

        @pl.when(z < 3)
        def _():
            finished_last(d).wait_send()

        @pl.when(partner(d) < 6)
        def _():
            finished_last(d).wait_recv()


def per_device(working, factor_panel):
    dma = pltpu.SemaphoreType.DMA
    gram, finished = pl.pallas_call(
        kernel,
        out_shape=[
            pltpu.VMEM((8, BLK, 8, 1, HALF), F32),
            pltpu.VMEM((4, 8, BLK, 1, HALF), F32),
        ],
        in_specs=[pl.BlockSpec(memory_space=pl.ANY)] * 2,
        out_specs=[pl.BlockSpec(memory_space=pltpu.VMEM)] * 2,
        scratch_shapes=[
            pltpu.VMEM((NJ, 2, BLK, HALF), F32),
            pltpu.VMEM((NJ, 2, BLK, HALF), F32),
            pltpu.VMEM((4, NJ, 2, BLK, HALF), F32),
            pltpu.VMEM((2, NJ, 2, BLK, HALF), F32),
            pltpu.VMEM((2 * BLK, 8 * HALF), BF16),
            pltpu.VMEM((2 * BLK, 8 * HALF), BF16),
            pltpu.VMEM((2, 8, BLK, HALF), F32),
            pltpu.VMEM((NJ, 2, BLK, HALF), F32),
            pltpu.VMEM((BLK, BLK), F32),
            pltpu.VMEM((BLK, BLK), F32),
            pltpu.VMEM((BLK, BLK), F32),
            dma((10,)),
            dma((8,)), dma((8,)), dma((8,)), dma((8,)),
            dma((4,)),
            dma((NJ,)), dma((NJ,)),
            dma((2, NJ)), dma((NJ,)),
            dma((NJ,)),
            dma((4, 4, NJ)), dma((4, NJ)),
            dma((2, NJ)), dma((2, NJ)),
            dma((2, 8)),
        ],
        compiler_params=pltpu.CompilerParams(
            collective_id=0, has_side_effects=True, vmem_limit_bytes=44 * 2**20
        ),
        cost_estimate=pl.CostEstimate(
            flops=3 * 2**31, bytes_accessed=20 * 2**20, transcendentals=0
        ),
        name="window",
    )(working.reshape(8, BLK, 8, 1, HALF), factor_panel)
    return gram.reshape(8, 1, BLK, 4, 1, BLK), finished.reshape(4, 8, BLK, 1, 1, HALF)


def solution(mesh):
    placed = (P(None, "row", None, None, "col", None), P(None, None, "row", None, None))
    return jax.shard_map(
        per_device,
        mesh=mesh,
        in_specs=placed,
        out_specs=(
            P(None, "row", None, None, "col", None),
            P(None, None, None, "col", "row", None),
        ),
        check_vma=False,
    )
```

time: 441 us -> 171 us (0.39); the launches traced: 433 us -> 169 us
  waiting for transfers between devices: 185 us -> 0 us
  Pallas kernels: 0 us -> 163 us
  local copies, waits for them, and re-layouts: 117 us -> 5.41 us
  matrix products: 57.9 us -> 0 us
  other arithmetic: 49.8 us -> 0 us
  between operations: 15.5 us -> 0.64 us
  starting transfers between devices: 6.78 us -> 0 us
    pallas_call x0 -> x1, Pallas kernels: none -> 163 us  [per_device(): pl.pallas_call(kernel, out_shape=[pltpu.VMEM((8, BLK, 8, 1, HALF), F32),...]
    all_gather x3 -> x0, waiting for transfers between devices: 137 us -> none  [the longest x2 71.6 us: picked(): lax.all_gather(value, axis)]
    dot_general x4 -> x0, matrix products: 54.2 us -> none  [the longest x3 36.7 us: eliminate(): jnp.einsum('rab,bc->rac', column_part, solved, precision=lax.Precision.HI...]
    all_to_all x1 -> x0, waiting for transfers between devices: 48.3 us -> none  [per_device(): lax.all_to_all(finished, 'row', split_axis=4, concat_axis=1, tiled=True)]
    another operation x6 -> x0, other arithmetic: 42.5 us -> none  [solve_row(): lax.linalg.triangular_solve(diagonal, slab, left_side=True, lower=True)]
    all_gather x1 -> x0, local copies, waits for them, and re-layouts: 28.3 us -> none  [per_device(): lax.all_gather(stacked.reshape(depth, blocks_cols, 1, width), 'col', axis...]
    unnamed x7 -> x2, local copies, waits for them, and re-layouts: 32.5 us -> 5.41 us
    dynamic_slice x6 -> x0, local copies, waits for them, and re-layouts: 21.8 us -> none  [the longest x2 17.6 us: per_device(): chosen = lax.dynamic_index_in_dim(gathered, row_index, 3, keepdims=False)]
  transfers between devices with their start and end apart: 4 -> 0, of which waited for: 4 -> 0; matrix products, arithmetic and copies ran while one was open for 24% -> 0% of each run, Pallas kernels for 0% -> 0%
where the time goes in v1:
time: 171 us; the launch traced here: 169 us
  Pallas kernels  163 us (95%)
  local copies, waits for them, and re-layouts  5.41 us (3%)
    pallas_call x1, Pallas kernels, per_device(): pl.pallas_call(kernel, out_shape=[pltpu.VMEM((8, BLK, 8, 1, HALF), F32),...  163 us
    unnamed x2, local copies, waits for them, and re-layouts  5.41 us

profile of v1, /device:TPU:32, one launch (start us, length us, event | category | flops | bytes accessed | tf_op | source)
XLA Modules:
  0.0 168.8 jit_solution(13832027192909522368)
XLA Ops:
  0.6 162.8 %window.1 = (f32[8,256,8,1,128]{4,3,2,1,0:T(1,128)S(1)}, f32[4,8,256,1,128]{4,3,2,1,0:T(1,128)S(1)}) custom-call(f32[8,256,8,1,128]{4,3,2,1,0:T(1,128)} %bitcast.7, f32[2,8,1,256,256]{4,3,2,1,0:T(8,128)} %f_ref.1), custom_call_target="tpu_custom_call" | custom-call | flops 6442450944 | bytes 20971520 | tf_op jit(solution)/shard_map/window/pallas_call | solution.py:389
  163.4 3.4 %copy.8 = f32[8,1,256,4,1,256]{5,4,3,2,1,0:T(1,128)} copy(f32[8,1,256,4,1,256]{5,4,3,2,1,0:T(1,128)S(1)} %bitcast.5) | data formatting | bytes 16777216
  166.8 2.0 %copy.9 = f32[4,8,256,1,1,128]{5,4,3,2,1,0:T(1,128)} copy(f32[4,8,256,1,1,128]{5,4,3,2,1,0:T(1,128)S(1)} %bitcast.6) | data formatting | bytes 8388608

commit v2 on v1

v2 whole, which is shorter than its diff:
```python
import jax
import jax.numpy as jnp
from jax import lax
from jax.experimental import pallas as pl
from jax.experimental.pallas import tpu as pltpu
from jax.sharding import PartitionSpec as P

MESH = pl.DeviceIdType.MESH
F32 = jnp.float32
BF16 = jnp.bfloat16
BLK = 256
HALF = 128
PARTS = 1
ROWS = BLK // PARTS
NQ = 8 * PARTS
LAG = 2
STEPS = NQ + 4 * LAG
EARLY = 0
AFTER = NQ
PACE = 28
SLOT = 3
SCALE = 1.0 / 512


def full(a, b):
    return lax.dot_general(
        a, b, (((1,), (0,)), ((), ())), precision=lax.Precision.HIGHEST, preferred_element_type=F32
    )


def small_inverse(block):
    row = lax.broadcasted_iota(jnp.int32, (HALF, HALF), 0)
    col = lax.broadcasted_iota(jnp.int32, (HALF, HALF), 1)
    eye = row == col
    on_diagonal = jnp.where(eye, block, 0.0)
    inv_col = 1.0 / jnp.sum(on_diagonal, axis=1, keepdims=True)
    inv_row = 1.0 / jnp.sum(on_diagonal, axis=0, keepdims=True)
    first = (row == col + 1) & ((row & 1) == 1)
    inverse = jnp.where(eye, inv_col, jnp.where(first, -block * inv_col * inv_row, 0.0))
    shift = 1
    while (1 << shift) < HALF:
        below = ((row >> shift) & 1) == 1
        beside = (col >> shift) == (row >> shift) - 1
        lower = jnp.where(below & beside, block, 0.0)
        inverse = inverse - full(inverse, full(lower, inverse))
        shift += 1
    return inverse


def split(value):
    high = value.astype(BF16)
    low = (value - high.astype(F32)).astype(BF16)
    return high, low


def tdot(a, b):
    return lax.dot_general(a, b, (((0,), (0,)), ((), ())), preferred_element_type=F32)


def kernel(
    w_ref, f_ref, gram_ref, fin_ref,
    own, oth, panel, cross, high, low, stage, slab, diag, lower, inv,
    load_sem, a2a_send, a2a_recv, local_sem,
    oth_send, oth_recv, own_send, own_recv, copy_sem,
    dir_send, panel_recv, cross_send, cross_recv, stage_sem,
):
    r = lax.axis_index("row")
    c = lax.axis_index("col")
    z, k = lax.div(r, 2), lax.rem(r, 2)
    y, x = lax.div(c, 4), lax.rem(c, 4)
    dx = lax.rem(x + 4 - 2 * lax.rem(z, 2), 4)
    dy = lax.rem(y + 4 - lax.div(z, 2), 4)
    other = (r + 1 - 2 * k, c)
    right = (r, 4 * y + lax.rem(x + 1, 4))
    left = (r, 4 * y + lax.rem(x + 3, 4))
    up = (r, 4 * lax.rem(y + 1, 4) + x)
    down = (r, 4 * lax.rem(y + 3, 4) + x)
    is_top = z == 3
    is_source = lax.div(lax.rem(c, 8), 2) == z
    source_panel = 2 * lax.rem(c, 2) + lax.div(c, 8)

    def remote(src, dst, send, recv, device):
        return pltpu.make_async_remote_copy(
            src, dst, send, recv, device_id=device, device_id_type=MESH
        )

    def loads():
        found = [pltpu.make_async_copy(f_ref.at[k, SLOT, 0], diag, load_sem.at[8])]
        found.append(pltpu.make_async_copy(f_ref.at[0, SLOT, 0], lower, load_sem.at[9]))
        for s in range(8):
            found.append(
                pltpu.make_async_copy(
                    w_ref.at[SLOT, :, s, 0, :], slab.at[s], load_sem.at[s]
                )
            )
        return found

    @pl.when(is_top)
    def _():
        for copy in loads():
            copy.start()

    barrier = pltpu.get_barrier_semaphore()
    for d in range(1, 8):
        pl.semaphore_signal(
            barrier, inc=1, device_id=(lax.rem(r + d, 8), c), device_id_type=MESH
        )
    for device in (right, left, up, down):
        pl.semaphore_signal(barrier, inc=1, device_id=device, device_id_type=MESH)
    pl.semaphore_wait(barrier, 11)

    def finished(m, source):
        d, f = 1 + lax.rem(m, 7), lax.div(m, 7)
        t = r ^ d
        origin = t if source else r
        return (
            (f < SLOT) | (origin < 6),
            remote(
                w_ref.at[f, :, t], fin_ref.at[f, r], a2a_send.at[m], a2a_recv.at[m], (t, c)
            ),
        )

    def start_finished(m, early):
        go, copy = finished(m, False)
        d = 1 + lax.rem(m, 7)
        free = (z == 1) | (lax.div(r ^ d, 2) == 3) | (d == 1) | (m < EARLY)

        @pl.when(go & (free if early else jnp.logical_not(free)))
        def _():
            copy.start()

    def start_early(m, carry):
        start_finished(m, True)
        return carry

    lax.fori_loop(0, 28, start_early, 0)

    own_rows = pltpu.make_async_copy(
        w_ref.at[pl.ds(0, 3), :, r], fin_ref.at[pl.ds(0, 3), r], local_sem.at[0]
    )
    own_last = pltpu.make_async_copy(
        w_ref.at[pl.ds(3, 1), :, r], fin_ref.at[pl.ds(3, 1), r], local_sem.at[1]
    )
    own_rows.start()

    @pl.when(z < 3)
    def _():
        own_last.start()

    @pl.when(is_top)
    def _():
        for copy in loads():
            copy.wait()
        top = small_inverse(diag[0:HALF, 0:HALF])
        bottom = small_inverse(diag[HALF:BLK, HALF:BLK])
        inv[0:HALF, 0:HALF] = top
        inv[0:HALF, HALF:BLK] = jnp.zeros((HALF, HALF), F32)
        inv[HALF:BLK, HALF:BLK] = bottom
        inv[HALF:BLK, 0:HALF] = -full(bottom, full(diag[HALF:BLK, 0:HALF], top))

    def part(ref, q):
        if PARTS == 1:
            return ref.at[q]
        return ref.at[lax.div(q, PARTS), pl.ds(pl.multiple_of(lax.rem(q, PARTS) * ROWS, ROWS), ROWS), :]

    def to_other(q):
        return remote(part(own, q), part(oth, q), oth_send.at[q], oth_recv.at[q], other)

    def down_ring(q, target, sem):
        return remote(
            part(own, q), part(own, q), own_send.at[sem, q], own_recv.at[q], (2 * target + k, c)
        )

    def forwards_ring(q):
        return ((z == 0) & (lax.rem(q, 2) == 0)) | ((z == 2) & (lax.rem(q, 2) == 1))

    def to_panel(q):
        return pltpu.make_async_copy(part(own, q), part(panel.at[source_panel], q), copy_sem.at[q])

    def solved_chunk(q):
        @pl.when(is_top)
        def _():
            @pl.when(k == 1)
            def _():
                to_other(q).wait_recv()

            @pl.when(lax.rem(q, PARTS) == PARTS - 1)
            def _():
                s = lax.div(q, PARTS)

                @pl.when(k == 1)
                def _():
                    slab[s] = slab[s] - full(lower[...], oth[s])

                own[s] = full(inv[...], slab[s])

        @pl.when(z < 3)
        def _():
            down_ring(q, 1, 0).wait_recv()

    def send_solved(q):
        @pl.when(is_source)
        def _():
            to_panel(q).start()

        to_other(q).start()

        @pl.when(is_top)
        def _():
            down_ring(q, 0, 0).start()
            down_ring(q, 2, 1).start()

        @pl.when(forwards_ring(q))
        def _():
            down_ring(q, 1, 0).start()

    def hops(kp, b, q):
        odd = lax.rem(kp + q, 2)
        x_active = (k == 1) | (dy == 2 * b)
        y_active = (k == 0) | (dx == kp)
        return (
            (x_active & ((dx == kp) | ((kp == 1) & (dx == 2))), right),
            (x_active & ((dx == kp) | ((kp == 0) & (dx == 3))), left),
            (
                y_active
                & (
                    (dy == 2 * b)
                    | ((odd == 0) & (dy == 1) & (b == 0))
                    | ((odd == 1) & (dy == 3) & (b == 1))
                ),
                up,
            ),
            (
                y_active
                & (
                    (dy == 2 * b)
                    | ((odd == 0) & (dy == 1) & (b == 1))
                    | ((odd == 1) & (dy == 3) & (b == 0))
                ),
                down,
            ),
        )

    def hop(src, p, q, i, device):
        return remote(
            part(src, q), part(panel.at[p], q), dir_send.at[i, p, q], panel_recv.at[p, q], device
        )

    def to_cross(src, b, q):
        return remote(
            part(src, q), part(cross.at[b], q), cross_send.at[b, q], cross_recv.at[b, q], other
        )

    def start_all(src, kp, b, q):
        for i, (go, device) in enumerate(hops(kp, b, q)):
            @pl.when(go)
            def _(i=i, device=device):
                hop(src, 2 * kp + b, q, i, device).start()

        @pl.when(kp != k)
        def _():
            to_cross(src, b, q).start()

    def distance(kp, b):
        ex = lax.rem(dx + 4 - kp, 4)
        ey = lax.rem(dy + 4 - 2 * b, 4)
        return jnp.minimum(ex, 4 - ex) + jnp.minimum(ey, 4 - ey)

    def pass_on(kp, b, t):
        far = distance(kp, b)
        q = t - LAG * far

        @pl.when((far > 0) & (q >= 0) & (q < NQ))
        def _():
            p = 2 * kp + b
            hop(panel.at[p], p, q, 0, right).wait_recv()
            start_all(panel.at[p], kp, b, q)

    def staged(i, s):
        slot = i & 1
        return pltpu.make_async_copy(
            stage.at[slot, s], gram_ref.at[i, :, s, 0, :], stage_sem.at[slot, s]
        )

    def split_columns():
        @pl.when(jnp.logical_not(is_top & (k == 1)))
        def _():
            for q in range(NQ):
                to_other(q).wait_recv()

        for s in range(8):
            at = slice(HALF * s, HALF * (s + 1))
            high[0:BLK, at], low[0:BLK, at] = split(own[s])
            high[BLK:, at], low[BLK:, at] = split(oth[s])

    def gram_block(j, b):
        i = 2 * j + b
        p = 2 * k + b
        for n in range(2 * PARTS):
            to_cross(own, b, 2 * PARTS * j + n).wait_recv()
        mine = jnp.concatenate([panel[p, 2 * j], panel[p, 2 * j + 1]], axis=1)
        theirs = jnp.concatenate([cross[b, 2 * j], cross[b, 2 * j + 1]], axis=1)
        a_high, a_low = split(jnp.concatenate([mine, theirs], axis=0))

        @pl.when(i >= 2)
        def _():
            for s in range(8):
                staged(i, s).wait()

        for q in range(4):
            at = slice(BLK * q, BLK * (q + 1))
            b_high, b_low = high[:, at], low[:, at]
            value = (tdot(a_low, b_high) + tdot(a_high, b_low)) + tdot(a_high, b_high)
            value = value * SCALE
            stage[i & 1, 2 * q] = value[:, :HALF]
            stage[i & 1, 2 * q + 1] = value[:, HALF:]
            staged(i, 2 * q).start()
            staged(i, 2 * q + 1).start()

    def step(t, carry):
        @pl.when(t < NQ)
        def _():
            solved_chunk(t)

            @pl.when(is_source)
            def _():
                start_all(own, lax.rem(c, 2), lax.div(c, 8), t)

            send_solved(t)

        for kp in range(2):
            for b in range(2):
                pass_on(kp, b, t)

        def start_late(m, carry):
            start_finished(m, False)
            return carry

        first = EARLY + PACE * (t - AFTER)
        lax.fori_loop(
            jnp.where(t < AFTER, 28, jnp.minimum(first, 28)),
            jnp.where(t == STEPS - 1, 28, jnp.minimum(first + PACE, 28)),
            start_late,
            0,
        )
        return carry

    lax.fori_loop(0, STEPS, step, 0)

    @pl.when(is_source)
    def _():
        for q in range(NQ):
            to_panel(q).wait()

    split_columns()
    last = [
        pltpu.make_async_copy(
            own.at[r], fin_ref.at[SLOT, 6 + k, :, 0, :], local_sem.at[2]
        ),
        pltpu.make_async_copy(
            oth.at[r], fin_ref.at[SLOT, 7 - k, :, 0, :], local_sem.at[3]
        ),
    ]
    for copy in last:
        copy.start()

    def product(j, carry):
        gram_block(j, 0)
        gram_block(j, 1)
        return carry

    lax.fori_loop(0, 4, product, 0)

    for i in (6, 7):
        for s in range(8):
            staged(i, s).wait()
    for copy in last:
        copy.wait()
    own_rows.wait()

    @pl.when(z < 3)
    def _():
        own_last.wait()

    def close(q, carry):
        to_other(q).wait_send()

        @pl.when(is_top)
        def _():
            down_ring(q, 0, 0).wait_send()
            down_ring(q, 2, 1).wait_send()

        @pl.when(forwards_ring(q))
        def _():
            down_ring(q, 1, 0).wait_send()

        for kp in range(2):
            for b in range(2):
                for i, (go, device) in enumerate(hops(kp, b, q)):
                    @pl.when(go)
                    def _(i=i, p=2 * kp + b, device=device):
                        hop(panel.at[p], p, q, i, device).wait_send()
        for b in range(2):
            to_cross(own, b, q).wait_send()
        return carry

    lax.fori_loop(0, NQ, close, 0)

    def close_finished(m, carry):
        go, copy = finished(m, False)

        @pl.when(go)
        def _():
            copy.wait_send()

        go, copy = finished(m, True)

        @pl.when(go)
        def _():
            copy.wait_recv()

        return carry

    lax.fori_loop(0, 28, close_finished, 0)


def per_device(working, factor_panel):
    dma = pltpu.SemaphoreType.DMA
    gram, finished = pl.pallas_call(
        kernel,
        out_shape=[
            pltpu.VMEM((8, BLK, 8, 1, HALF), F32),
            pltpu.VMEM((4, 8, BLK, 1, HALF), F32),
        ],
        in_specs=[pl.BlockSpec(memory_space=pl.ANY)] * 2,
        out_specs=[pl.BlockSpec(memory_space=pltpu.VMEM)] * 2,
        scratch_shapes=[
            pltpu.VMEM((8, BLK, HALF), F32),
            pltpu.VMEM((8, BLK, HALF), F32),
            pltpu.VMEM((4, 8, BLK, HALF), F32),
            pltpu.VMEM((2, 8, BLK, HALF), F32),
            pltpu.VMEM((2 * BLK, 8 * HALF), BF16),
            pltpu.VMEM((2 * BLK, 8 * HALF), BF16),
            pltpu.VMEM((2, 8, BLK, HALF), F32),
            pltpu.VMEM((8, BLK, HALF), F32),
            pltpu.VMEM((BLK, BLK), F32),
            pltpu.VMEM((BLK, BLK), F32),
            pltpu.VMEM((BLK, BLK), F32),
            dma((10,)),
            dma((28,)), dma((28,)),
            dma((4,)),
            dma((NQ,)), dma((NQ,)),
            dma((2, NQ)), dma((NQ,)),
            dma((NQ,)),
            dma((4, 4, NQ)), dma((4, NQ)),
            dma((2, NQ)), dma((2, NQ)),
            dma((2, 8)),
        ],
        compiler_params=pltpu.CompilerParams(
            collective_id=0, has_side_effects=True, vmem_limit_bytes=44 * 2**20
        ),
        cost_estimate=pl.CostEstimate(
            flops=3 * 2**31, bytes_accessed=20 * 2**20, transcendentals=0
        ),
        name="window",
    )(working.reshape(8, BLK, 8, 1, HALF), factor_panel)
    return gram.reshape(8, 1, BLK, 4, 1, BLK), finished.reshape(4, 8, BLK, 1, 1, HALF)


def solution(mesh):
    placed = (P(None, "row", None, None, "col", None), P(None, None, "row", None, None))
    return jax.shard_map(
        per_device,
        mesh=mesh,
        in_specs=placed,
        out_specs=(
            P(None, "row", None, None, "col", None),
            P(None, None, None, "col", "row", None),
        ),
        check_vma=False,
    )
```

time: 171 us -> 101 us (0.59); the launches traced: 169 us -> 101 us
  Pallas kernels: 163 us -> 95.2 us
    pallas_call x1, Pallas kernels: 163 us -> 95.2 us  [per_device(): pl.pallas_call(kernel, out_shape=[pltpu.VMEM((8, BLK, 8, 1, HALF), F32),...]
where the time goes in v2:
time: 101 us
  Pallas kernels  95.2 us (94%)
  local copies, waits for them, and re-layouts  5.41 us (5%)
    pallas_call x1, Pallas kernels, per_device(): pl.pallas_call(kernel, out_shape=[pltpu.VMEM((8, BLK, 8, 1, HALF), F32),...  95.2 us
    unnamed x2, local copies, waits for them, and re-layouts  5.41 us

profile of v2, /device:TPU:32, one launch (start us, length us, event | category | flops | bytes accessed | tf_op | source)
XLA Modules:
  0.0 101.3 jit_solution(6516805045517906143)
XLA Ops:
  0.6 95.2 %window.1 = (f32[8,256,8,1,128]{4,3,2,1,0:T(1,128)S(1)}, f32[4,8,256,1,128]{4,3,2,1,0:T(1,128)S(1)}) custom-call(f32[8,256,8,1,128]{4,3,2,1,0:T(1,128)} %bitcast.7, f32[2,8,1,256,256]{4,3,2,1,0:T(8,128)} %f_ref.1), custom_call_target="tpu_custom_call" | custom-call | flops 6442450944 | bytes 20971520 | tf_op jit(solution)/shard_map/window/pallas_call | solution.py:429
  95.9 3.4 %copy.8 = f32[8,1,256,4,1,256]{5,4,3,2,1,0:T(1,128)} copy(f32[8,1,256,4,1,256]{5,4,3,2,1,0:T(1,128)S(1)} %bitcast.5) | data formatting | bytes 16777216
  99.3 2.0 %copy.9 = f32[4,8,256,1,1,128]{5,4,3,2,1,0:T(1,128)} copy(f32[4,8,256,1,1,128]{5,4,3,2,1,0:T(1,128)S(1)} %bitcast.6) | data formatting | bytes 8388608

commit v3 on v2

--- a/solution.py
+++ b/solution.py
@@ -110,7 +110,7 @@
     pl.semaphore_wait(barrier, 11)
 
     def finished(m, source):
-        d, f = 1 + lax.rem(m, 7), lax.div(m, 7)
+        d, f = 1 + lax.rem(m + 3, 7), lax.div(m, 7)
         t = r ^ d
         origin = t if source else r
         return (
@@ -122,7 +122,7 @@
 
     def start_finished(m, early):
         go, copy = finished(m, False)
-        d = 1 + lax.rem(m, 7)
+        d = 1 + lax.rem(m + 3, 7)
         free = (z == 1) | (lax.div(r ^ d, 2) == 3) | (d == 1) | (m < EARLY)
 
         @pl.when(go & (free if early else jnp.logical_not(free)))

time: 101 us -> 104 us (1.030)
  Pallas kernels: 95.2 us -> 97.5 us
    pallas_call x1, Pallas kernels: 95.2 us -> 97.5 us  [per_device(): pl.pallas_call(kernel, out_shape=[pltpu.VMEM((8, BLK, 8, 1, HALF), F32),...]
where the time goes in v3:
time: 104 us
  Pallas kernels  97.5 us (94%)
  local copies, waits for them, and re-layouts  5.41 us (5%)
    pallas_call x1, Pallas kernels, per_device(): pl.pallas_call(kernel, out_shape=[pltpu.VMEM((8, BLK, 8, 1, HALF), F32),...  97.5 us
    unnamed x2, local copies, waits for them, and re-layouts  5.41 us

profile of v3, /device:TPU:32, one launch (start us, length us, event | category | flops | bytes accessed | tf_op | source)
XLA Modules:
  0.0 103.6 jit_solution(4981766234161496687)
XLA Ops:
  0.6 97.5 %window.1 = (f32[8,256,8,1,128]{4,3,2,1,0:T(1,128)S(1)}, f32[4,8,256,1,128]{4,3,2,1,0:T(1,128)S(1)}) custom-call(f32[8,256,8,1,128]{4,3,2,1,0:T(1,128)} %bitcast.7, f32[2,8,1,256,256]{4,3,2,1,0:T(8,128)} %f_ref.1), custom_call_target="tpu_custom_call" | custom-call | flops 6442450944 | bytes 20971520 | tf_op jit(solution)/shard_map/window/pallas_call | solution.py:429
  98.2 3.4 %copy.8 = f32[8,1,256,4,1,256]{5,4,3,2,1,0:T(1,128)} copy(f32[8,1,256,4,1,256]{5,4,3,2,1,0:T(1,128)S(1)} %bitcast.5) | data formatting | bytes 16777216
  101.6 2.0 %copy.9 = f32[4,8,256,1,1,128]{5,4,3,2,1,0:T(1,128)} copy(f32[4,8,256,1,1,128]{5,4,3,2,1,0:T(1,128)S(1)} %bitcast.6) | data formatting | bytes 8388608
